TPU v7x, 32 devices: a whole 2x2x4 slice. The times are simulated.
32 devices in a mesh: dp: 8 (over y, x, core), seq: 4 (over z).
Axes of the slice: x: 2, y: 2, z: 4, core: 2. Of those that a mesh axis runs over, the one named last changes fastest.
Arguments:
- tokens: bfloat16 [16, 1024, 512], P('dp', 'seq'), may hold values from -6 to 6
- memory: bfloat16 [16, 1024, 512], P('dp', 'seq'), may hold values from -6 to 6
- tgt_segments: int32 [16, 1024], P('dp'), may hold values from 0 to 2, as said below
- mem_segments: int32 [16, 1024], P('dp'), may hold values from 0 to 2, as said below
- cotangent: bfloat16 [16, 1024, 512], P('dp', 'seq'), may hold values from -6 to 6
- w_qkv: bfloat16 [512, 1536], replicated, may hold values from -0.25 to 0.25
- w_self_out: bfloat16 [512, 512], replicated, may hold values from -1.5 to 1.5
- w_cross_q: bfloat16 [512, 512], replicated, may hold values from -0.25 to 0.25
- w_cross_kv: bfloat16 [512, 1024], replicated, may hold values from -0.25 to 0.25
- w_cross_out: bfloat16 [512, 512], replicated, may hold values from -1.5 to 1.5
- w_up: bfloat16 [512, 2048], replicated, may hold values from -0.25 to 0.25
- w_down: bfloat16 [2048, 512], replicated, may hold values from -0.125 to 0.125
- ln1_gain: float32 [512], replicated, may hold values from 0.25 to 1.75
- ln1_bias: float32 [512], replicated, may hold values from -1.8 to 1.8
- ln2_gain: float32 [512], replicated, may hold values from 0.25 to 1.75
- ln2_bias: float32 [512], replicated, may hold values from -1.8 to 1.8
- ln3_gain: float32 [512], replicated, may hold values from 0.25 to 1.75
- ln3_bias: float32 [512], replicated, may hold values from -1.8 to 1.8
Outputs:
- output: bfloat16 [16, 1024, 512], P('dp', 'seq')
- grad_tokens: float32 [16, 1024, 512], P('dp', 'seq')
- grad_memory: float32 [16, 1024, 512], P('dp', 'seq')
- grad_w_qkv: float32 [512, 1536], replicated
- grad_w_self_out: float32 [512, 512], replicated
- grad_w_cross_q: float32 [512, 512], replicated
- grad_w_cross_kv: float32 [512, 1024], replicated
- grad_w_cross_out: float32 [512, 512], replicated
- grad_w_up: float32 [512, 2048], replicated
- grad_w_down: float32 [2048, 512], replicated
- grad_ln1_gain: float32 [512], replicated
- grad_ln1_bias: float32 [512], replicated
- grad_ln2_gain: float32 [512], replicated
- grad_ln2_bias: float32 [512], replicated
- grad_ln3_gain: float32 [512], replicated
- grad_ln3_bias: float32 [512], replicated
Inputs may be any that keep to these rules, and one draw needn't show every extreme that they name: `tgt_segments`: along a row the ids never fall and all three occur; document 1 begins within the row's first 256 positions and ends within its last 256. `mem_segments`: along a row the ids never fall and all three occur.
All inputs are finite; a program needn't handle non-finite values.
Results may differ from a plain program's by a relative error of at most 0.02.
Values may be sent and summed in bfloat16 or wider, within the bound.
No kernel may reach another device: no remote copies, remote signals or barrier semaphores. Data moves between devices by JAX's collectives and lax.ppermute only.
A program may use at most 128 MiB of HBM per device.

v0:
```python
import math
import jax
import jax.numpy as jnp
from jax import lax
from jax.sharding import PartitionSpec as P

HEAD_DIM = 64


def mat_dot(left, right):
    return jnp.dot(left, right, preferred_element_type=jnp.float32)


def left_dot(left, right):
    return lax.dot_general(
        left, right, (((0,), (0,)), ((), ())), preferred_element_type=jnp.float32
    )


def right_dot(left, right):
    return lax.dot_general(
        left, right, (((1,), (1,)), ((), ())), preferred_element_type=jnp.float32
    )


def layer_norm(values, gain, bias):
    centre = values - jnp.mean(values, axis=-1, keepdims=True)
    recip = lax.rsqrt(jnp.mean(centre * centre, axis=-1, keepdims=True) + 1e-05)
    normed = centre * recip
    return (normed * gain + bias, normed, recip)


def norm_back(grad_out, normed, recip, gain):
    grad_gain = jnp.sum(grad_out * normed, axis=0)
    grad_bias = jnp.sum(grad_out, axis=0)
    scaled = grad_out * gain
    grad_in = recip * (
        scaled
        - jnp.mean(scaled, axis=-1, keepdims=True)
        - normed * jnp.mean(scaled * normed, axis=-1, keepdims=True)
    )
    return (grad_in, grad_gain, grad_bias)


def causal_mask(segment_row):
    place = jnp.arange(segment_row.shape[0])
    return (place[None, :] <= place[:, None]) & (segment_row[:, None] == segment_row[None, :])


def cross_mask(tgt_row, mem_row):
    return tgt_row[:, None] == mem_row[None, :]


def masked_scores(queries, key_heads, allowed, score_scale):
    scores = (
        jnp.einsum("qhd,khd->hqk", queries, key_heads, preferred_element_type=jnp.float32)
        * score_scale
    )
    return jnp.where(allowed[None], scores, -1000000000.0)


def attend_forward(queries, key_heads, value_heads, allowed, score_scale):
    scores = masked_scores(queries, key_heads, allowed, score_scale)
    highest = jnp.max(scores, axis=-1, keepdims=True)
    expo = jnp.exp(scores - highest)
    total = jnp.sum(expo, axis=-1, keepdims=True)
    probs = (expo / total).astype(jnp.bfloat16)
    context = jnp.einsum("hqk,khd->qhd", probs, value_heads, preferred_element_type=jnp.float32)
    return (context.astype(jnp.bfloat16), highest + jnp.log(total))


def attend_backward(queries, key_heads, value_heads, log_total, d_context, allowed, score_scale):
    scores = masked_scores(queries, key_heads, allowed, score_scale)
    probs = jnp.exp(scores - log_total)
    d_values = jnp.einsum(
        "hqk,qhd->khd", probs.astype(jnp.bfloat16), d_context, preferred_element_type=jnp.float32
    ).astype(jnp.bfloat16)
    d_probs = jnp.einsum("qhd,khd->hqk", d_context, value_heads, preferred_element_type=jnp.float32)
    centre = jnp.sum(probs * d_probs, axis=-1, keepdims=True)
    d_scores = (probs * (d_probs - centre)).astype(jnp.bfloat16)
    d_queries = (
        jnp.einsum("hqk,khd->qhd", d_scores, key_heads, preferred_element_type=jnp.float32)
        * score_scale
    ).astype(jnp.bfloat16)
    d_keys = (
        jnp.einsum("hqk,qhd->khd", d_scores, queries, preferred_element_type=jnp.float32)
        * score_scale
    ).astype(jnp.bfloat16)
    return (d_queries, d_keys, d_values)


def body(
    tokens,
    memory,
    tgt_segments,
    mem_segments,
    cotangent,
    w_qkv,
    w_self_out,
    w_cross_q,
    w_cross_kv,
    w_cross_out,
    w_up,
    w_down,
    ln1_gain,
    ln1_bias,
    ln2_gain,
    ln2_bias,
    ln3_gain,
    ln3_bias,
):
    row_count, tok_local, model_width = tokens.shape
    mem_local = memory.shape[1]
    seq_parts = lax.axis_size("seq")
    head_share = model_width // seq_parts
    heads_here = head_share // HEAD_DIM
    seq_len = tgt_segments.shape[1]
    mem_len = mem_segments.shape[1]
    score_scale = 1.0 / math.sqrt(HEAD_DIM)
    token_total = row_count * tok_local
    flat_tokens = tokens.reshape(token_total, model_width)
    flat_memory = memory.reshape(row_count * mem_local, model_width)
    mixed_proj = (
        mat_dot(flat_tokens, w_qkv)
        .astype(jnp.bfloat16)
        .reshape(row_count, tok_local, 3, seq_parts, head_share)
    )
    self_heads = lax.all_to_all(mixed_proj, "seq", split_axis=3, concat_axis=1, tiled=True).reshape(
        row_count, seq_len, 3, heads_here, HEAD_DIM
    )
    memory_proj = (
        mat_dot(flat_memory, w_cross_kv)
        .astype(jnp.bfloat16)
        .reshape(row_count, mem_local, 2, seq_parts, head_share)
    )
    memory_heads = lax.all_to_all(
        memory_proj, "seq", split_axis=3, concat_axis=1, tiled=True
    ).reshape(row_count, mem_len, 2, heads_here, HEAD_DIM)
    self_q = self_heads[:, :, 0]
    self_k = self_heads[:, :, 1]
    self_v = self_heads[:, :, 2]
    memory_k = memory_heads[:, :, 0]
    memory_v = memory_heads[:, :, 1]

    def self_forward(row_item):
        queries, key_heads, value_heads, segment_row = row_item
        return attend_forward(
            queries, key_heads, value_heads, causal_mask(segment_row), score_scale
        )

    self_context, self_lse = lax.map(self_forward, (self_q, self_k, self_v, tgt_segments))
    self_back = lax.all_to_all(
        self_context.reshape(row_count, seq_len, 1, head_share),
        "seq",
        split_axis=1,
        concat_axis=2,
        tiled=True,
    )
    context_one = self_back.reshape(token_total, model_width)
    attn_one = mat_dot(context_one, w_self_out)
    norm_one, normed_one, recip_one = layer_norm(
        flat_tokens.astype(jnp.float32) + attn_one, ln1_gain, ln1_bias
    )
    norm_one_low = norm_one.astype(jnp.bfloat16)
    cross_proj = (
        mat_dot(norm_one_low, w_cross_q)
        .astype(jnp.bfloat16)
        .reshape(row_count, tok_local, 1, seq_parts, head_share)
    )
    cross_q = lax.all_to_all(cross_proj, "seq", split_axis=3, concat_axis=1, tiled=True).reshape(
        row_count, seq_len, heads_here, HEAD_DIM
    )

    def cross_forward(row_item):
        queries, key_heads, value_heads, tgt_row, mem_row = row_item
        return attend_forward(
            queries, key_heads, value_heads, cross_mask(tgt_row, mem_row), score_scale
        )

    cross_context, cross_lse = lax.map(
        cross_forward, (cross_q, memory_k, memory_v, tgt_segments, mem_segments)
    )
    cross_back = lax.all_to_all(
        cross_context.reshape(row_count, seq_len, 1, head_share),
        "seq",
        split_axis=1,
        concat_axis=2,
        tiled=True,
    )
    context_two = cross_back.reshape(token_total, model_width)
    attn_two = mat_dot(context_two, w_cross_out)
    norm_two, normed_two, recip_two = layer_norm(norm_one + attn_two, ln2_gain, ln2_bias)
    norm_two_low = norm_two.astype(jnp.bfloat16)
    pre_act = mat_dot(norm_two_low, w_up)
    sigma = jax.nn.sigmoid(pre_act)
    hidden_low = (pre_act * sigma).astype(jnp.bfloat16)
    fed = mat_dot(hidden_low, w_down)
    result, normed_three, recip_three = layer_norm(norm_two + fed, ln3_gain, ln3_bias)
    output = result.astype(jnp.bfloat16).reshape(row_count, tok_local, model_width)
    grad_out = cotangent.reshape(token_total, model_width).astype(jnp.float32)
    d_resid_three, d_gain_three, d_bias_three = norm_back(
        grad_out, normed_three, recip_three, ln3_gain
    )
    d_fed_low = d_resid_three.astype(jnp.bfloat16)
    grad_down = left_dot(hidden_low, d_fed_low)
    d_hidden = right_dot(d_fed_low, w_down)
    d_pre_low = (d_hidden * sigma * (1.0 + pre_act * (1.0 - sigma))).astype(jnp.bfloat16)
    grad_up = left_dot(norm_two_low, d_pre_low)
    d_norm_two = d_resid_three + right_dot(d_pre_low, w_up)
    d_resid_two, d_gain_two, d_bias_two = norm_back(d_norm_two, normed_two, recip_two, ln2_gain)
    d_attn_two = d_resid_two.astype(jnp.bfloat16)
    grad_cross_out = left_dot(context_two, d_attn_two)
    d_context_two = (
        right_dot(d_attn_two, w_cross_out)
        .astype(jnp.bfloat16)
        .reshape(row_count, tok_local, seq_parts, head_share)
    )
    d_cross_heads = lax.all_to_all(
        d_context_two, "seq", split_axis=2, concat_axis=1, tiled=True
    ).reshape(row_count, seq_len, heads_here, HEAD_DIM)

    def cross_backward(row_item):
        queries, key_heads, value_heads, log_total, d_context, tgt_row, mem_row = row_item
        return attend_backward(
            queries,
            key_heads,
            value_heads,
            log_total,
            d_context,
            cross_mask(tgt_row, mem_row),
            score_scale,
        )

    d_cross_q, d_mem_keys, d_mem_values = lax.map(
        cross_backward,
        (cross_q, memory_k, memory_v, cross_lse, d_cross_heads, tgt_segments, mem_segments),
    )
    d_memory_kv = jnp.stack((d_mem_keys, d_mem_values), axis=2).reshape(
        row_count, mem_len, 2, 1, head_share
    )
    back_query, back_memory = (
        lax.all_to_all(
            d_cross_q.reshape(row_count, seq_len, 1, 1, head_share),
            "seq",
            split_axis=1,
            concat_axis=3,
            tiled=True,
        ),
        lax.all_to_all(d_memory_kv, "seq", split_axis=1, concat_axis=3, tiled=True),
    )
    d_query_flat = back_query.reshape(token_total, model_width)
    d_memory_flat = back_memory.reshape(row_count * mem_local, 2 * model_width)
    grad_cross_q = left_dot(norm_one_low, d_query_flat)
    grad_cross_kv = left_dot(flat_memory, d_memory_flat)
    grad_memory = right_dot(d_memory_flat, w_cross_kv).reshape(row_count, mem_local, model_width)
    d_norm_one = d_resid_two + right_dot(d_query_flat, w_cross_q)
    d_resid_one, d_gain_one, d_bias_one = norm_back(d_norm_one, normed_one, recip_one, ln1_gain)
    d_attn_one = d_resid_one.astype(jnp.bfloat16)
    grad_self_out = left_dot(context_one, d_attn_one)
    d_context_one = (
        right_dot(d_attn_one, w_self_out)
        .astype(jnp.bfloat16)
        .reshape(row_count, tok_local, seq_parts, head_share)
    )
    d_self_heads = lax.all_to_all(
        d_context_one, "seq", split_axis=2, concat_axis=1, tiled=True
    ).reshape(row_count, seq_len, heads_here, HEAD_DIM)

    def self_backward(row_item):
        queries, key_heads, value_heads, log_total, d_context, segment_row = row_item
        return attend_backward(
            queries,
            key_heads,
            value_heads,
            log_total,
            d_context,
            causal_mask(segment_row),
            score_scale,
        )

    d_self_q, d_self_k, d_self_v = lax.map(
        self_backward, (self_q, self_k, self_v, self_lse, d_self_heads, tgt_segments)
    )
    d_mixed = jnp.stack((d_self_q, d_self_k, d_self_v), axis=2).reshape(
        row_count, seq_len, 3, 1, head_share
    )
    back_mixed = lax.all_to_all(d_mixed, "seq", split_axis=1, concat_axis=3, tiled=True).reshape(
        token_total, 3 * model_width
    )
    grad_qkv = left_dot(flat_tokens, back_mixed)
    grad_tokens = (d_resid_one + right_dot(back_mixed, w_qkv)).reshape(
        row_count, tok_local, model_width
    )
    summed = lax.psum(
        (
            grad_qkv,
            grad_self_out,
            grad_cross_q,
            grad_cross_kv,
            grad_cross_out,
            grad_up,
            grad_down,
            d_gain_one,
            d_bias_one,
            d_gain_two,
            d_bias_two,
            d_gain_three,
            d_bias_three,
        ),
        ("dp", "seq"),
    )
    return (
        output,
        grad_tokens,
        grad_memory,
        summed[0],
        summed[1],
        summed[2],
        summed[3],
        summed[4],
        summed[5],
        summed[6],
        summed[7],
        summed[8],
        summed[9],
        summed[10],
        summed[11],
        summed[12],
    )


def solution(mesh):
    return jax.shard_map(
        body,
        mesh=mesh,
        in_specs=(
            P("dp", "seq", None),
            P("dp", "seq", None),
            P("dp", None),
            P("dp", None),
            P("dp", "seq", None),
            P(),
            P(),
            P(),
            P(),
            P(),
            P(),
            P(),
            P(),
            P(),
            P(),
            P(),
            P(),
            P(),
        ),
        out_specs=(
            P("dp", "seq", None),
            P("dp", "seq", None),
            P("dp", "seq", None),
            P(),
            P(),
            P(),
            P(),
            P(),
            P(),
            P(),
            P(),
            P(),
            P(),
            P(),
            P(),
            P(),
        ),
        check_vma=False,
    )
```

profile of v0, /device:TPU:0, one launch (start us, length us, event | category | flops | bytes accessed | tf_op | source)
XLA Modules:
  0.0 717.0 jit_solution(7663693203559814328)
XLA Ops:
  7.2 3.8 convolution_convert_fusion
  11.0 3.9 reshape.401
  17.9 6.3 all-to-all-start
  24.2 37.1 %all-to-all-done = bf16[2,256,3,4,128]{4,1,2,0,3:T(8,128)(2,1)} async-done(((bf16[2,256,3,4,128]{4,1,2,0,3:T(8,128)(2,1)}), bf16[2,256,3,4,128]{4,1,2,0,3:T(8,128)(2,1)}, u32[]{:S(2)}, u32[]{:S(2)}) %all-to-all-start) | async-done | bytes 1572896 | tf_op jit(solution)/shard_map/all_to_all | solution.py:128
  61.3 3.8 copy.197
  65.0 3.8 reshape.402
  72.0 16.4 %while.52 = (s32[]{:T(128)}, bf16[2,1024,2,64]{1,3,2,0:T(8,128)(2,1)}, f32[2,2,1024,1]{2,1,3,0:T(2,128)S(1)}, bf16[2,1024,2,64]{1,3,2,0:T(8,128)(2,1)}, s32[2,10...) while((s32[]{:T(128)}, ...), condition=%wide.region_3.4_spmd, body=%wide.region_0.3_spmd.sunk | while | flops 565311488 | bytes 36780216 | solution.py:151
  90.7 4.1 all-to-all-start.1
  103.5 5.4 all-to-all-done.1
  108.9 4.3 all-to-all-start.2
  122.7 15.7 %all-to-all-done.2 = bf16[2,256,2,4,128]{4,2,1,0,3:T(2,128)(2,1)} async-done(((bf16[2,256,2,4,128]{4,2,1,0,3:T(2,128)(2,1)}), bf16[2,256,2,4,128]{4,2,1,0,3:T(2,128)(2,1)}, u32[]{:S(2)}, u32[]{:S(2)}) %all-to-all-start.2) | async-done | bytes 1048608 | tf_op jit(solution)/shard_map/all_to_all | solution.py:136
  138.4 4.4 all-to-all-start.3
  142.9 3.8 copy.202
  151.5 5.4 all-to-all-done.3
  162.1 18.5 %while.53 = (s32[]{:T(128)}, bf16[2,1024,2,64]{1,3,2,0:T(8,128)(2,1)}, f32[2,2,1024,1]{2,1,3,0:T(2,128)S(1)}, bf16[2,1024,2,64]{1,3,2,0:T(8,128)(2,1)}, s32[2,10...) while((s32[]{:T(128)}, ...), condition=%wide.region_9.10_spmd, body=%wide.region_6.9_spmd.sunk | while | flops 563214336 | bytes 36792512 | solution.py:180
  182.6 4.8 all-to-all-start.4
  189.4 12.1 %all-to-all-done.4 = bf16[2,1024,1,128]{3,0,2,1:T(2,128)(2,1)} async-done(((bf16[2,1024,1,128]{3,0,2,1:T(2,128)(2,1)}), bf16[2,1024,1,128]{3,0,2,1:T(2,128)(2,1)}, u32[]{:S(2)}, u32[]{:S(2)}) %all-to-all-start.4) | async-done | bytes 524320 | tf_op jit(solution)/shard_map/all_to_all | solution.py:183
  221.2 4.3 all-to-all-start.5
  225.5 14.1 %all-to-all-done.5 = bf16[2,256,4,128]{3,1,0,2:T(8,128)(2,1)} async-done(((bf16[2,256,4,128]{3,1,0,2:T(8,128)(2,1)}), bf16[2,256,4,128]{3,1,0,2:T(8,128)(2,1)}, u32[]{:S(2)}, u32[]{:S(2)}) %all-to-all-start.5) | async-done | bytes 524320 | tf_op jit(solution)/shard_map/all_to_all | solution.py:218
  246.6 27.1 %while.54 = (s32[]{:T(128)}, bf16[2,1024,2,64]{1,3,2,0:T(8,128)(2,1)}, bf16[2,1024,2,64]{1,3,2,0:T(8,128)(2,1)}, bf16[2,1024,2,64]{1,3,2,0:T(8,128)(2,1)}, bf16[...) while((s32[]{:T(128)}, ...), condition=%wide.region_20.21_spmd, body=%wide.region_18.20_spmd.sunk | while | flops 1375336448 | bytes 86594928 | solution.py:234
  275.1 16.4 %all_to_all.150 = bf16[2,1024,1,1,128]{4,0,3,2,1:T(2,128)(2,1)S(1)} all-to-all(bf16[2,1024,1,1,128]{4,0,3,2,1:T(2,128)(2,1)S(1)} %copy.210), channel_id=1, replica_groups=mesh['dp'=8,'seq'=4] {'seq'}, dimensions={1} | all-to-all | bytes 1048576 | tf_op jit(solution)/shard_map/all_to_all | solution.py:242
  296.0 4.1 all-to-all-start.7
  303.5 10.2 %all-to-all-done.7 = bf16[2,256,4,128]{3,1,0,2:T(8,128)(2,1)} async-done(((bf16[2,256,4,128]{3,1,0,2:T(8,128)(2,1)}), bf16[2,256,4,128]{3,1,0,2:T(8,128)(2,1)}, u32[]{:S(2)}, u32[]{:S(2)}) %all-to-all-start.7) | async-done | bytes 524320 | tf_op jit(solution)/shard_map/all_to_all | solution.py:265
  313.7 4.5 all-to-all-start.9
  323.4 27.0 %while.55 = (s32[]{:T(128)}, bf16[2,1024,2,64]{1,3,2,0:T(8,128)(2,1)}, bf16[2,1024,2,64]{1,3,2,0:T(8,128)(2,1)}, bf16[2,1024,2,64]{1,3,2,0:T(8,128)(2,1)}, bf16[...) while((s32[]{:T(128)}, ...), condition=%wide.region_25.26_spmd, body=%wide.region_23.25_spmd.sunk | while | flops 1377433600 | bytes 86582632 | solution.py:281
  353.2 5.0 copy.215
  358.2 5.1 all-to-all-start.8
  366.2 5.2 fusion.153
  383.1 16.2 %all-to-all-done.8 = bf16[2,1024,3,1,128]{4,0,3,2,1:T(2,128)(2,1)} async-done(((bf16[2,1024,3,1,128]{4,0,3,2,1:T(2,128)(2,1)}), bf16[2,1024,3,1,128]{4,0,3,2,1:T(2,128)(2,1)}, u32[]{:S(2)}, u32[]{:S(2)}) %all-to-all-start.8) | async-done | bytes 1572896 | tf_op jit(solution)/shard_map/all_to_all | solution.py:287
  409.5 40.1 %all-reduce = (f32[512]{0:T(512)}, f32[512]{0:T(512)}, f32[512]{0:T(512)}, f32[512]{0:T(512)}, f32[512]{0:T(512)}, /*index=5*/f32[512]{0:T(512)}) all-reduce(f32[512]{0:T(512)S(1)} %get-tuple-element.334, f32[512]{0:T(512)S(1)} %get-tuple-element.341, f32[512]{0:T(512)S(1)} %copy-done.74, ...), channel_id=1, replica_groups=mesh['dp'=8,'seq'=4] {'dp','seq'}, use_global_device_ids=true, to_apply=%region_34.35 | all-reduce | flops 3072 | bytes 24576 | tf_op jit(solution)/shard_map/psum | solution.py:294
  454.5 3.8 convolution_add_fusion.3
  458.3 234.8 %all-reduce.4.cloned.1.call-done = (f32[512,1536]{0,1:T(8,128)}, f32[512,512]{1,0:T(8,128)}, f32[512,512]{1,0:T(8,128)}, f32[512,1024]{0,1:T(8,128)}, f32[512,51...) async-done(((f32[512,1536]{0,1:T(8,128)}, f32[512,512]{1,0:T(8,128)}, f32[512,512]{1,0:T(8,128)}, f32[512,1024]{0,1:T(8,128)}, f32[512,512]{1,0:T(8,128)}, ...) | async-done | bytes 16777232 | tf_op jit(solution)/shard_map/psum | solution.py:294
  (357 shorter events, 218.6 us)
Async XLA Ops:
  7.2 198.6 %copy-start = (bf16[512,2048]{1,0:T(8,128)(2,1)S(1)}, bf16[512,2048]{1,0:T(8,128)(2,1)}, u32[]{:S(2)}) copy-start(bf16[512,2048]{1,0:T(8,128)(2,1)} %param.36) | copy-start | bytes 6291460
  17.9 43.4 %all-to-all-start = ((bf16[2,256,3,4,128]{4,1,2,0,3:T(8,128)(2,1)}), bf16[2,256,3,4,128]{4,1,2,0,3:T(8,128)(2,1)}, u32[]{:S(2)}, u32[]{:S(2)}) async-start(bf16[2,256,3,4,128]{4,1,2,0,3:T(8,128)(2,1)} %copy.196), calls=%async_computation | async-start | bytes 3145728 | tf_op jit(solution)/shard_map/all_to_all | solution.py:128
  88.4 15.1 %copy-start.5 = (bf16[2,1024,2,64]{1,3,2,0:T(8,128)(2,1)}, bf16[2,1024,2,64]{1,3,2,0:T(8,128)(2,1)S(1)}, u32[]{:S(2)}) copy-start(bf16[2,1024,2,64]{1,3,2,0:T(8,128)(2,1)S(1)} %get-tuple-element.855) | copy-start | bytes 1572868
  88.4 15.1 %copy-start.7 = (bf16[2,1024,2,64]{1,3,2,0:T(8,128)(2,1)}, bf16[2,1024,2,64]{1,3,2,0:T(8,128)(2,1)S(1)}, u32[]{:S(2)}) copy-start(bf16[2,1024,2,64]{1,3,2,0:T(8,128)(2,1)S(1)} %get-tuple-element.856) | copy-start | bytes 1572868
  88.4 15.1 %copy-start.59 = (f32[2,2,1024,1]{2,1,3,0:T(2,128)}, f32[2,2,1024,1]{2,1,3,0:T(2,128)S(1)}, u32[]{:S(2)}) copy-start(f32[2,2,1024,1]{2,1,3,0:T(2,128)S(1)} %get-tuple-element.796) | copy-start | bytes 49156
  90.7 18.2 %all-to-all-start.1 = ((bf16[2,1024,1,128]{3,0,2,1:T(2,128)(2,1)}), bf16[2,1024,1,128]{3,0,2,1:T(2,128)(2,1)}, u32[]{:S(2)}, u32[]{:S(2)}) async-start(bf16[2,1024,1,128]{3,0,2,1:T(2,128)(2,1)} %copy.198), calls=%async_computation.1 | async-start | bytes 1048576 | tf_op jit(solution)/shard_map/all_to_all | solution.py:152
  103.5 14.1 %copy-start.70 = (f32[512]{0:T(512)S(1)}, f32[512]{0:T(512)}, u32[]{:S(2)}) copy-start(f32[512]{0:T(512)} %param.38) | copy-start | bytes 6148
  103.5 14.1 %copy-start.76 = (f32[512]{0:T(512)S(1)}, f32[512]{0:T(512)}, u32[]{:S(2)}) copy-start(f32[512]{0:T(512)} %param.39) | copy-start | bytes 6148
  108.9 29.5 %all-to-all-start.2 = ((bf16[2,256,2,4,128]{4,2,1,0,3:T(2,128)(2,1)}), bf16[2,256,2,4,128]{4,2,1,0,3:T(2,128)(2,1)}, u32[]{:S(2)}, u32[]{:S(2)}) async-start(bf16[2,256,2,4,128]{4,2,1,0,3:T(2,128)(2,1)} %copy.201), calls=%async_computation.2 | async-start | bytes 2097152 | tf_op jit(solution)/shard_map/all_to_all | solution.py:136
  138.4 18.5 %all-to-all-start.3 = ((bf16[2,256,1,4,128]{4,1,0,2,3:T(8,128)(2,1)}), bf16[2,256,1,4,128]{4,1,0,2,3:T(8,128)(2,1)}, u32[]{:S(2)}, u32[]{:S(2)}) async-start(bf16[2,256,1,4,128]{4,1,0,2,3:T(8,128)(2,1)} %copy.203), calls=%async_computation.3 | async-start | bytes 1048576 | tf_op jit(solution)/shard_map/all_to_all | solution.py:170
  142.9 19.2 %copy-start.58 = (s32[2,1024]{1,0:T(2,128)S(1)}, s32[2,1024]{1,0:T(2,128)}, u32[]{:S(2)}) copy-start(s32[2,1024]{1,0:T(2,128)} %param.29) | copy-start | bytes 24580
  162.1 25.4 %copy-start.69 = (f32[512]{0:T(512)S(1)}, f32[512]{0:T(512)}, u32[]{:S(2)}) copy-start(f32[512]{0:T(512)} %param.42) | copy-start | bytes 6148
  182.6 23.2 %copy-start.65 = (f32[512]{0:T(512)S(1)}, f32[512]{0:T(512)}, u32[]{:S(2)}) copy-start(f32[512]{0:T(512)} %param.40) | copy-start | bytes 6148
  182.6 23.2 %copy-start.67 = (f32[512]{0:T(512)S(1)}, f32[512]{0:T(512)}, u32[]{:S(2)}) copy-start(f32[512]{0:T(512)} %param.41) | copy-start | bytes 6148
  182.6 18.9 %all-to-all-start.4 = ((bf16[2,1024,1,128]{3,0,2,1:T(2,128)(2,1)}), bf16[2,1024,1,128]{3,0,2,1:T(2,128)(2,1)}, u32[]{:S(2)}, u32[]{:S(2)}) async-start(bf16[2,1024,1,128]{3,0,2,1:T(2,128)(2,1)} %copy.205), calls=%async_computation.4 | async-start | bytes 1048576 | tf_op jit(solution)/shard_map/all_to_all | solution.py:183
  216.0 29.8 %copy-start.10 = (f32[512,512]{1,0:T(8,128)}, f32[512,512]{1,0:T(8,128)S(1)}, u32[]{:S(2)}) copy-start(f32[512,512]{1,0:T(8,128)S(1)} %subtract_multiply_fusion.1) | copy-start | bytes 3145732
  216.0 30.6 %copy-start.4 = (bf16[2,1024,2,64]{1,3,2,0:T(8,128)(2,1)S(1)}, bf16[2,1024,2,64]{1,3,2,0:T(8,128)(2,1)}, u32[]{:S(2)}) copy-start(bf16[2,1024,2,64]{1,3,2,0:T(8,128)(2,1)} %get-tuple-element.854) | copy-start | bytes 1572868
  216.0 30.6 %copy-start.9 = (bf16[2,1024,2,64]{1,3,2,0:T(8,128)(2,1)S(1)}, bf16[2,1024,2,64]{1,3,2,0:T(8,128)(2,1)}, u32[]{:S(2)}) copy-start(bf16[2,1024,2,64]{1,3,2,0:T(8,128)(2,1)} %get-tuple-element.857) | copy-start | bytes 1572868
  221.2 18.4 %all-to-all-start.5 = ((bf16[2,256,4,128]{3,1,0,2:T(8,128)(2,1)}), bf16[2,256,4,128]{3,1,0,2:T(8,128)(2,1)}, u32[]{:S(2)}, u32[]{:S(2)}) async-start(bf16[2,256,4,128]{3,1,0,2:T(8,128)(2,1)} %copy.208), calls=%async_computation.5 | async-start | bytes 1048576 | tf_op jit(solution)/shard_map/all_to_all | solution.py:218
  273.7 18.3 %copy-start.11 = (f32[512,512]{1,0:T(8,128)S(1)}, f32[512,512]{1,0:T(8,128)}, u32[]{:S(2)}) copy-start(f32[512,512]{1,0:T(8,128)} %copy-done.10) | copy-start | bytes 3145732
  296.0 17.8 %all-to-all-start.7 = ((bf16[2,256,4,128]{3,1,0,2:T(8,128)(2,1)}), bf16[2,256,4,128]{3,1,0,2:T(8,128)(2,1)}, u32[]{:S(2)}, u32[]{:S(2)}) async-start(bf16[2,256,4,128]{3,1,0,2:T(8,128)(2,1)} %copy.213), calls=%async_computation.7 | async-start | bytes 1048576 | tf_op jit(solution)/shard_map/all_to_all | solution.py:265
  301.4 21.9 %copy-start.6 = (bf16[2,1024,2,64]{1,3,2,0:T(8,128)(2,1)S(1)}, bf16[2,1024,2,64]{1,3,2,0:T(8,128)(2,1)}, u32[]{:S(2)}) copy-start(bf16[2,1024,2,64]{1,3,2,0:T(8,128)(2,1)} %copy-done.5) | copy-start | bytes 1572868
  301.4 21.9 %copy-start.8 = (bf16[2,1024,2,64]{1,3,2,0:T(8,128)(2,1)S(1)}, bf16[2,1024,2,64]{1,3,2,0:T(8,128)(2,1)}, u32[]{:S(2)}) copy-start(bf16[2,1024,2,64]{1,3,2,0:T(8,128)(2,1)} %copy-done.7) | copy-start | bytes 1572868
  301.5 21.9 %copy-start.60 = (f32[2,2,1024,1]{2,1,3,0:T(2,128)S(1)}, f32[2,2,1024,1]{2,1,3,0:T(2,128)}, u32[]{:S(2)}) copy-start(f32[2,2,1024,1]{2,1,3,0:T(2,128)} %copy-done.59) | copy-start | bytes 49156
  313.7 44.5 %all-to-all-start.9 = ((bf16[2,1024,2,1,128]{4,0,3,2,1:T(2,128)(2,1)}), bf16[2,1024,2,1,128]{4,0,3,2,1:T(2,128)(2,1)}, u32[]{:S(2)}, u32[]{:S(2)}) async-start(bf16[2,1024,2,1,128]{4,0,3,2,1:T(2,128)(2,1)} %copy.218), calls=%async_computation.9 | async-start | bytes 2097152 | tf_op jit(solution)/shard_map/all_to_all | solution.py:249
  350.4 13.3 %copy-start.12 = (f32[512,512]{1,0:T(8,128)S(1)}, f32[512,512]{1,0:T(8,128)}, u32[]{:S(2)}) copy-start(f32[512,512]{1,0:T(8,128)} %copy-done.10) | copy-start | bytes 3145732
  353.2 13.0 %copy-start.64 = (f32[512]{0:T(512)S(1)}, f32[512]{0:T(512)}, u32[]{:S(2)}) copy-start(f32[512]{0:T(512)} %copy-done.63) | copy-start | bytes 6148
  353.2 13.0 %copy-start.66 = (f32[512]{0:T(512)S(1)}, f32[512]{0:T(512)}, u32[]{:S(2)}) copy-start(f32[512]{0:T(512)} %param.40) | copy-start | bytes 6148
  353.2 13.0 %copy-start.68 = (f32[512]{0:T(512)S(1)}, f32[512]{0:T(512)}, u32[]{:S(2)}) copy-start(f32[512]{0:T(512)} %param.41) | copy-start | bytes 6148
  358.2 41.1 %all-to-all-start.8 = ((bf16[2,1024,3,1,128]{4,0,3,2,1:T(2,128)(2,1)}), bf16[2,1024,3,1,128]{4,0,3,2,1:T(2,128)(2,1)}, u32[]{:S(2)}, u32[]{:S(2)}) async-start(bf16[2,1024,3,1,128]{4,0,3,2,1:T(2,128)(2,1)} %copy.215), calls=%async_computation.8 | async-start | bytes 3145728 | tf_op jit(solution)/shard_map/all_to_all | solution.py:287
  363.3 329.8 %all-reduce.4.cloned.1.call-start = ((), (), s32[]{:S(2)}) async-start(), calls=%async_computation.10 | async-start | bytes 33554432 | tf_op jit(solution)/shard_map/psum | solution.py:294
  383.1 23.1 %copy-start.51 = (bf16[2,256,512]{2,1,0:T(8,128)(2,1)S(1)}, bf16[2,256,512]{2,1,0:T(8,128)(2,1)}, u32[]{:S(2)}) copy-start(bf16[2,256,512]{2,1,0:T(8,128)(2,1)} %param.26) | copy-start | bytes 1572868
  (79 other events, 247.0 us)
Sparse Core Ops, SparseCore 0:
  409.0 284.0 all-reduce.3
where the time goes:
time: 728 us; the launch traced here: 717 us
  waiting for transfers between devices  351 us (48%)
  local copies, waits for them, and re-layouts  112 us (15%)
  matrix products  105 us (14%)
  blocking collectives  56.5 us (8%)
  starting transfers between devices  42.4 us (6%)
  other arithmetic  33.6 us (5%)
  between operations  14.9 us (2%)
    psum x1, waiting for transfers between devices, body(): lax.psum((grad_qkv, grad_self_out, grad_cross_q, grad_cross_kv, grad_cros...  235 us
    psum x1, blocking collectives, body(): lax.psum((grad_qkv, grad_self_out, grad_cross_q, grad_cross_kv, grad_cros...  40.1 us
    all_to_all x1, waiting for transfers between devices, body(): lax.all_to_all(mixed_proj, 'seq', split_axis=3, concat_axis=1, tiled=True)  37.1 us
    unnamed x122, local copies, waits for them, and re-layouts  19.7 us
    dot_general x7, matrix products, left_dot(): lax.dot_general(left, right, (((0,), (0,)), ((), ())), preferred_element_...  19 us
    all_to_all x1, blocking collectives, body(): lax.all_to_all(d_cross_q.reshape(row_count, seq_len, 1, 1, head_share), '...  16.4 us
    all_to_all x1, waiting for transfers between devices, body(): lax.all_to_all(d_mixed, 'seq', split_axis=1, concat_axis=3, tiled=True)  16.2 us
    all_to_all x1, waiting for transfers between devices, body(): lax.all_to_all(memory_proj, 'seq', split_axis=3, concat_axis=1, tiled=True)  15.7 us
  transfers between devices with their start and end apart: 10, of which 9 were waited for; matrix products, arithmetic and copies ran while one was open for 14% of the time, Pallas kernels for 0%

commit v1 on v0

--- a/solution.py
+++ b/solution.py
@@ -238,14 +238,17 @@
     d_memory_kv = jnp.stack((d_mem_keys, d_mem_values), axis=2).reshape(
         row_count, mem_len, 2, 1, head_share
     )
+
+    def limits_return_all(inputs):
+        return jnp.concatenate(
+            lax.all_to_all(
+                jnp.stack(jnp.split(inputs, lax.axis_size("seq"), axis=1), axis=0), "seq", 0, 0
+            ),
+            axis=3,
+        )
+
     back_query, back_memory = (
-        lax.all_to_all(
-            d_cross_q.reshape(row_count, seq_len, 1, 1, head_share),
-            "seq",
-            split_axis=1,
-            concat_axis=3,
-            tiled=True,
-        ),
+        limits_return_all(d_cross_q.reshape(row_count, seq_len, 1, 1, head_share)),
         lax.all_to_all(d_memory_kv, "seq", split_axis=1, concat_axis=3, tiled=True),
     )
     d_query_flat = back_query.reshape(token_total, model_width)

time: 728 us -> 730 us (level)
    unnamed x122 -> x116, local copies, waits for them, and re-layouts: 19.7 us -> 19.7 us
  transfers between devices with their start and end apart: 10 -> 10, of which waited for: 9 -> 9; matrix products, arithmetic and copies ran while one was open for 14% -> 13% of each run, Pallas kernels for 0% -> 0%
where the time goes in v1:
time: 730 us; the launch traced here: 719 us
  waiting for transfers between devices  352 us (48%)
  local copies, waits for them, and re-layouts  110 us (15%)
  matrix products  109 us (15%)
  blocking collectives  56.7 us (8%)
  starting transfers between devices  42.1 us (6%)
  other arithmetic  33.7 us (5%)
  between operations  14.9 us (2%)
    psum x1, waiting for transfers between devices, body(): lax.psum((grad_qkv, grad_self_out, grad_cross_q, grad_cross_kv, grad_cros...  235 us
    psum x1, blocking collectives, body(): lax.psum((grad_qkv, grad_self_out, grad_cross_q, grad_cross_kv, grad_cros...  40.1 us
    all_to_all x1, waiting for transfers between devices, body(): lax.all_to_all(mixed_proj, 'seq', split_axis=3, concat_axis=1, tiled=True)  37.1 us
    unnamed x116, local copies, waits for them, and re-layouts  19.7 us
    dot_general x7, matrix products, left_dot(): lax.dot_general(left, right, (((0,), (0,)), ((), ())), preferred_element_...  19 us
    dot_general x8, matrix products, masked_scores(): jnp.einsum('qhd,khd->hqk', queries, key_heads, preferred_element_type=jnp...  16.9 us
    all_to_all x1, blocking collectives, limits_return_all(): lax.all_to_all(jnp.stack(jnp.split(inputs, lax.axis_size('seq'), axis=1),...  16.6 us
    all_to_all x1, waiting for transfers between devices, body(): lax.all_to_all(d_mixed, 'seq', split_axis=1, concat_axis=3, tiled=True)  16.2 us
  transfers between devices with their start and end apart: 10, of which 9 were waited for; matrix products, arithmetic and copies ran while one was open for 13% of the time, Pallas kernels for 0%

profile of v1, /device:TPU:0, one launch (start us, length us, event | category | flops | bytes accessed | tf_op | source)
XLA Modules:
  0.0 719.2 jit_solution(12766187297644499975)
XLA Ops:
  7.2 3.8 convolution_convert_fusion
  11.0 3.9 reshape.400
  17.9 6.3 all-to-all-start
  24.2 37.1 %all-to-all-done = bf16[2,256,3,4,128]{4,1,2,0,3:T(8,128)(2,1)} async-done(((bf16[2,256,3,4,128]{4,1,2,0,3:T(8,128)(2,1)}), bf16[2,256,3,4,128]{4,1,2,0,3:T(8,128)(2,1)}, u32[]{:S(2)}, u32[]{:S(2)}) %all-to-all-start) | async-done | bytes 1572896 | tf_op jit(solution)/shard_map/all_to_all | solution.py:128
  61.3 3.8 copy.208
  65.0 3.8 reshape.401
  72.2 18.4 %while.52 = (s32[]{:T(128)}, bf16[2,1024,2,64]{1,3,2,0:T(8,128)(2,1)}, f32[2,2,1024,1]{2,1,3,0:T(2,128)S(1)}, bf16[2,1024,2,64]{1,3,2,0:T(8,128)(2,1)}, s32[2,10...) while((s32[]{:T(128)}, ...), condition=%wide.region_3.4_spmd, body=%wide.region_0.3_spmd.sunk | while | flops 565311488 | bytes 36780216 | solution.py:151
  92.6 4.1 all-to-all-start.1
  103.4 7.4 %all-to-all-done.1 = bf16[2,1024,1,128]{3,0,2,1:T(2,128)(2,1)} async-done(((bf16[2,1024,1,128]{3,0,2,1:T(2,128)(2,1)}), bf16[2,1024,1,128]{3,0,2,1:T(2,128)(2,1)}, u32[]{:S(2)}, u32[]{:S(2)}) %all-to-all-start.1) | async-done | bytes 524320 | tf_op jit(solution)/shard_map/all_to_all | solution.py:152
  110.8 4.2 all-to-all-start.2
  125.6 14.7 %all-to-all-done.2 = bf16[2,256,2,4,128]{4,2,1,0,3:T(2,128)(2,1)} async-done(((bf16[2,256,2,4,128]{4,2,1,0,3:T(2,128)(2,1)}), bf16[2,256,2,4,128]{4,2,1,0,3:T(2,128)(2,1)}, u32[]{:S(2)}, u32[]{:S(2)}) %all-to-all-start.2) | async-done | bytes 1048608 | tf_op jit(solution)/shard_map/all_to_all | solution.py:136
  140.3 4.4 all-to-all-start.3
  144.8 3.8 copy.213
  153.4 5.4 all-to-all-done.3
  164.0 18.5 %while.53 = (s32[]{:T(128)}, bf16[2,1024,2,64]{1,3,2,0:T(8,128)(2,1)}, f32[2,2,1024,1]{2,1,3,0:T(2,128)S(1)}, bf16[2,1024,2,64]{1,3,2,0:T(8,128)(2,1)}, s32[2,10...) while((s32[]{:T(128)}, ...), condition=%wide.region_9.10_spmd, body=%wide.region_6.9_spmd.sunk | while | flops 563214336 | bytes 36792512 | solution.py:180
  184.5 4.8 all-to-all-start.4
  191.3 12.1 %all-to-all-done.4 = bf16[2,1024,1,128]{3,0,2,1:T(2,128)(2,1)} async-done(((bf16[2,1024,1,128]{3,0,2,1:T(2,128)(2,1)}), bf16[2,1024,1,128]{3,0,2,1:T(2,128)(2,1)}, u32[]{:S(2)}, u32[]{:S(2)}) %all-to-all-start.4) | async-done | bytes 524320 | tf_op jit(solution)/shard_map/all_to_all | solution.py:183
  223.1 4.3 all-to-all-start.5
  227.4 14.0 %all-to-all-done.5 = bf16[2,256,4,128]{3,1,0,2:T(8,128)(2,1)} async-done(((bf16[2,256,4,128]{3,1,0,2:T(8,128)(2,1)}), bf16[2,256,4,128]{3,1,0,2:T(8,128)(2,1)}, u32[]{:S(2)}, u32[]{:S(2)}) %all-to-all-start.5) | async-done | bytes 524320 | tf_op jit(solution)/shard_map/all_to_all | solution.py:218
  248.4 27.1 %while.54 = (s32[]{:T(128)}, bf16[2,1024,2,64]{1,3,2,0:T(8,128)(2,1)}, bf16[2,1024,2,64]{1,3,2,0:T(8,128)(2,1)}, bf16[2,1024,2,64]{1,3,2,0:T(8,128)(2,1)}, bf16[...) while((s32[]{:T(128)}, ...), condition=%wide.region_20.21_spmd, body=%wide.region_18.20_spmd.sunk | while | flops 1375336448 | bytes 86594928 | solution.py:234
  277.4 16.6 %all_to_all.140 = bf16[4,2,256,1,1,128]{5,2,1,4,3,0:T(8,128)(2,1)S(1)} all-to-all(bf16[4,2,256,1,1,128]{5,2,1,4,3,0:T(8,128)(2,1)S(1)} %pad_maximum_fusion.2), channel_id=1, replica_groups=mesh['dp'=8,'seq'=4] {'seq'}, dimensions={0} | all-to-all | bytes 1048576 | tf_op jit(solution)/shard_map/all_to_all | solution.py:244
  298.4 4.1 all-to-all-start.7
  305.9 10.2 %all-to-all-done.7 = bf16[2,256,4,128]{3,1,0,2:T(8,128)(2,1)} async-done(((bf16[2,256,4,128]{3,1,0,2:T(8,128)(2,1)}), bf16[2,256,4,128]{3,1,0,2:T(8,128)(2,1)}, u32[]{:S(2)}, u32[]{:S(2)}) %all-to-all-start.7) | async-done | bytes 524320 | tf_op jit(solution)/shard_map/all_to_all | solution.py:268
  316.1 4.3 all-to-all-start.9
  325.5 27.0 %while.55 = (s32[]{:T(128)}, bf16[2,1024,2,64]{1,3,2,0:T(8,128)(2,1)}, bf16[2,1024,2,64]{1,3,2,0:T(8,128)(2,1)}, bf16[2,1024,2,64]{1,3,2,0:T(8,128)(2,1)}, bf16[...) while((s32[]{:T(128)}, ...), condition=%wide.region_25.26_spmd, body=%wide.region_23.25_spmd.sunk | while | flops 1377433600 | bytes 86582632 | solution.py:284
  355.3 5.1 copy.228
  360.4 5.1 all-to-all-start.8
  368.4 5.2 fusion.153
  385.3 16.2 %all-to-all-done.8 = bf16[2,1024,3,1,128]{4,0,3,2,1:T(2,128)(2,1)} async-done(((bf16[2,1024,3,1,128]{4,0,3,2,1:T(2,128)(2,1)}), bf16[2,1024,3,1,128]{4,0,3,2,1:T(2,128)(2,1)}, u32[]{:S(2)}, u32[]{:S(2)}) %all-to-all-start.8) | async-done | bytes 1572896 | tf_op jit(solution)/shard_map/all_to_all | solution.py:290
  411.7 40.1 %all-reduce = (f32[512]{0:T(512)}, f32[512]{0:T(512)}, f32[512]{0:T(512)}, f32[512]{0:T(512)}, f32[512]{0:T(512)}, /*index=5*/f32[512]{0:T(512)}) all-reduce(f32[512]{0:T(512)S(1)} %get-tuple-element.334, f32[512]{0:T(512)S(1)} %get-tuple-element.341, f32[512]{0:T(512)S(1)} %copy-done.71, ...), channel_id=1, replica_groups=mesh['dp'=8,'seq'=4] {'dp','seq'}, use_global_device_ids=true, to_apply=%region_34.35 | all-reduce | flops 3072 | bytes 24576 | tf_op jit(solution)/shard_map/psum | solution.py:297
  456.7 3.8 convolution_add_fusion.3
  460.5 234.7 %all-reduce.4.cloned.1.call-done = (f32[512,1536]{0,1:T(8,128)}, f32[512,512]{1,0:T(8,128)}, f32[512,512]{1,0:T(8,128)}, f32[512,1024]{0,1:T(8,128)}, f32[512,51...) async-done(((f32[512,1536]{0,1:T(8,128)}, f32[512,512]{1,0:T(8,128)}, f32[512,512]{1,0:T(8,128)}, f32[512,1024]{0,1:T(8,128)}, f32[512,512]{1,0:T(8,128)}, ...) | async-done | bytes 16777232 | tf_op jit(solution)/shard_map/psum | solution.py:297
  (355 shorter events, 219.8 us)
Async XLA Ops:
  7.2 200.5 %copy-start = (bf16[512,2048]{1,0:T(8,128)(2,1)S(1)}, bf16[512,2048]{1,0:T(8,128)(2,1)}, u32[]{:S(2)}) copy-start(bf16[512,2048]{1,0:T(8,128)(2,1)} %param.36) | copy-start | bytes 6291460
  17.9 43.4 %all-to-all-start = ((bf16[2,256,3,4,128]{4,1,2,0,3:T(8,128)(2,1)}), bf16[2,256,3,4,128]{4,1,2,0,3:T(8,128)(2,1)}, u32[]{:S(2)}, u32[]{:S(2)}) async-start(bf16[2,256,3,4,128]{4,1,2,0,3:T(8,128)(2,1)} %copy.207), calls=%async_computation | async-start | bytes 3145728 | tf_op jit(solution)/shard_map/all_to_all | solution.py:128
  90.6 12.8 %copy-start.56 = (f32[2,2,1024,1]{2,1,3,0:T(2,128)}, f32[2,2,1024,1]{2,1,3,0:T(2,128)S(1)}, u32[]{:S(2)}) copy-start(f32[2,2,1024,1]{2,1,3,0:T(2,128)S(1)} %get-tuple-element.800) | copy-start | bytes 49156
  92.6 18.2 %all-to-all-start.1 = ((bf16[2,1024,1,128]{3,0,2,1:T(2,128)(2,1)}), bf16[2,1024,1,128]{3,0,2,1:T(2,128)(2,1)}, u32[]{:S(2)}, u32[]{:S(2)}) async-start(bf16[2,1024,1,128]{3,0,2,1:T(2,128)(2,1)} %copy.209), calls=%async_computation.1 | async-start | bytes 1048576 | tf_op jit(solution)/shard_map/all_to_all | solution.py:152
  103.4 16.0 %copy-start.67 = (f32[512]{0:T(512)S(1)}, f32[512]{0:T(512)}, u32[]{:S(2)}) copy-start(f32[512]{0:T(512)} %param.38) | copy-start | bytes 6148
  103.4 16.0 %copy-start.73 = (f32[512]{0:T(512)S(1)}, f32[512]{0:T(512)}, u32[]{:S(2)}) copy-start(f32[512]{0:T(512)} %param.39) | copy-start | bytes 6148
  110.8 29.5 %all-to-all-start.2 = ((bf16[2,256,2,4,128]{4,2,1,0,3:T(2,128)(2,1)}), bf16[2,256,2,4,128]{4,2,1,0,3:T(2,128)(2,1)}, u32[]{:S(2)}, u32[]{:S(2)}) async-start(bf16[2,256,2,4,128]{4,2,1,0,3:T(2,128)(2,1)} %copy.212), calls=%async_computation.2 | async-start | bytes 2097152 | tf_op jit(solution)/shard_map/all_to_all | solution.py:136
  140.3 18.5 %all-to-all-start.3 = ((bf16[2,256,1,4,128]{4,1,0,2,3:T(8,128)(2,1)}), bf16[2,256,1,4,128]{4,1,0,2,3:T(8,128)(2,1)}, u32[]{:S(2)}, u32[]{:S(2)}) async-start(bf16[2,256,1,4,128]{4,1,0,2,3:T(8,128)(2,1)} %copy.214), calls=%async_computation.3 | async-start | bytes 1048576 | tf_op jit(solution)/shard_map/all_to_all | solution.py:170
  144.8 19.2 %copy-start.55 = (s32[2,1024]{1,0:T(2,128)S(1)}, s32[2,1024]{1,0:T(2,128)}, u32[]{:S(2)}) copy-start(s32[2,1024]{1,0:T(2,128)} %param.29) | copy-start | bytes 24580
  164.0 25.4 %copy-start.66 = (f32[512]{0:T(512)S(1)}, f32[512]{0:T(512)}, u32[]{:S(2)}) copy-start(f32[512]{0:T(512)} %param.42) | copy-start | bytes 6148
  184.5 23.2 %copy-start.62 = (f32[512]{0:T(512)S(1)}, f32[512]{0:T(512)}, u32[]{:S(2)}) copy-start(f32[512]{0:T(512)} %param.40) | copy-start | bytes 6148
  184.5 23.2 %copy-start.64 = (f32[512]{0:T(512)S(1)}, f32[512]{0:T(512)}, u32[]{:S(2)}) copy-start(f32[512]{0:T(512)} %param.41) | copy-start | bytes 6148
  184.5 18.9 %all-to-all-start.4 = ((bf16[2,1024,1,128]{3,0,2,1:T(2,128)(2,1)}), bf16[2,1024,1,128]{3,0,2,1:T(2,128)(2,1)}, u32[]{:S(2)}, u32[]{:S(2)}) async-start(bf16[2,1024,1,128]{3,0,2,1:T(2,128)(2,1)} %copy.216), calls=%async_computation.4 | async-start | bytes 1048576 | tf_op jit(solution)/shard_map/all_to_all | solution.py:183
  217.9 29.6 %copy-start.8 = (f32[512,512]{1,0:T(8,128)}, f32[512,512]{1,0:T(8,128)S(1)}, u32[]{:S(2)}) copy-start(f32[512,512]{1,0:T(8,128)S(1)} %subtract_multiply_fusion.1) | copy-start | bytes 3145732
  217.9 30.5 %copy-start.4 = (bf16[2,1024,2,64]{1,3,2,0:T(8,128)(2,1)S(1)}, bf16[2,1024,2,64]{1,3,2,0:T(8,128)(2,1)}, u32[]{:S(2)}) copy-start(bf16[2,1024,2,64]{1,3,2,0:T(8,128)(2,1)} %get-tuple-element.858) | copy-start | bytes 1572868
  217.9 30.5 %copy-start.7 = (bf16[2,1024,2,64]{1,3,2,0:T(8,128)(2,1)S(1)}, bf16[2,1024,2,64]{1,3,2,0:T(8,128)(2,1)}, u32[]{:S(2)}) copy-start(bf16[2,1024,2,64]{1,3,2,0:T(8,128)(2,1)} %get-tuple-element.861) | copy-start | bytes 1572868
  223.1 18.4 %all-to-all-start.5 = ((bf16[2,256,4,128]{3,1,0,2:T(8,128)(2,1)}), bf16[2,256,4,128]{3,1,0,2:T(8,128)(2,1)}, u32[]{:S(2)}, u32[]{:S(2)}) async-start(bf16[2,256,4,128]{3,1,0,2:T(8,128)(2,1)} %copy.219), calls=%async_computation.5 | async-start | bytes 1048576 | tf_op jit(solution)/shard_map/all_to_all | solution.py:218
  275.6 18.8 %copy-start.9 = (f32[512,512]{1,0:T(8,128)S(1)}, f32[512,512]{1,0:T(8,128)}, u32[]{:S(2)}) copy-start(f32[512,512]{1,0:T(8,128)} %copy-done.8) | copy-start | bytes 3145732
  298.4 17.8 %all-to-all-start.7 = ((bf16[2,256,4,128]{3,1,0,2:T(8,128)(2,1)}), bf16[2,256,4,128]{3,1,0,2:T(8,128)(2,1)}, u32[]{:S(2)}, u32[]{:S(2)}) async-start(bf16[2,256,4,128]{3,1,0,2:T(8,128)(2,1)} %copy.226), calls=%async_computation.7 | async-start | bytes 1048576 | tf_op jit(solution)/shard_map/all_to_all | solution.py:268
  303.8 21.7 %copy-start.5 = (bf16[2,1024,2,64]{1,3,2,0:T(8,128)(2,1)S(1)}, bf16[2,1024,2,64]{1,3,2,0:T(8,128)(2,1)}, u32[]{:S(2)}) copy-start(bf16[2,1024,2,64]{1,3,2,0:T(8,128)(2,1)} %get-tuple-element.859) | copy-start | bytes 1572868
  303.8 21.7 %copy-start.6 = (bf16[2,1024,2,64]{1,3,2,0:T(8,128)(2,1)S(1)}, bf16[2,1024,2,64]{1,3,2,0:T(8,128)(2,1)}, u32[]{:S(2)}) copy-start(bf16[2,1024,2,64]{1,3,2,0:T(8,128)(2,1)} %get-tuple-element.860) | copy-start | bytes 1572868
  303.9 21.7 %copy-start.57 = (f32[2,2,1024,1]{2,1,3,0:T(2,128)S(1)}, f32[2,2,1024,1]{2,1,3,0:T(2,128)}, u32[]{:S(2)}) copy-start(f32[2,2,1024,1]{2,1,3,0:T(2,128)} %copy-done.56) | copy-start | bytes 49156
  316.1 44.3 %all-to-all-start.9 = ((bf16[2,1024,2,1,128]{4,0,3,2,1:T(2,128)(2,1)}), bf16[2,1024,2,1,128]{4,0,3,2,1:T(2,128)(2,1)}, u32[]{:S(2)}, u32[]{:S(2)}) async-start(bf16[2,1024,2,1,128]{4,0,3,2,1:T(2,128)(2,1)} %copy.231), calls=%async_computation.9 | async-start | bytes 2097152 | tf_op jit(solution)/shard_map/all_to_all | solution.py:252
  352.5 13.3 %copy-start.10 = (f32[512,512]{1,0:T(8,128)S(1)}, f32[512,512]{1,0:T(8,128)}, u32[]{:S(2)}) copy-start(f32[512,512]{1,0:T(8,128)} %copy-done.8) | copy-start | bytes 3145732
  355.3 13.1 %copy-start.3 = (f32[512,512]{1,0:T(8,128)S(1)}, f32[512,512]{1,0:T(8,128)}, u32[]{:S(2)}) copy-start(f32[512,512]{1,0:T(8,128)} %copy-done.2) | copy-start | bytes 3145732
  355.3 13.1 %copy-start.59 = (f32[512]{0:T(512)S(1)}, f32[512]{0:T(512)}, u32[]{:S(2)}) copy-start(f32[512]{0:T(512)} %copy-done.58) | copy-start | bytes 6148
  355.3 13.1 %copy-start.61 = (f32[512]{0:T(512)S(1)}, f32[512]{0:T(512)}, u32[]{:S(2)}) copy-start(f32[512]{0:T(512)} %copy-done.60) | copy-start | bytes 6148
  355.3 13.1 %copy-start.63 = (f32[512]{0:T(512)S(1)}, f32[512]{0:T(512)}, u32[]{:S(2)}) copy-start(f32[512]{0:T(512)} %param.40) | copy-start | bytes 6148
  355.3 13.1 %copy-start.65 = (f32[512]{0:T(512)S(1)}, f32[512]{0:T(512)}, u32[]{:S(2)}) copy-start(f32[512]{0:T(512)} %param.41) | copy-start | bytes 6148
  360.4 41.0 %all-to-all-start.8 = ((bf16[2,1024,3,1,128]{4,0,3,2,1:T(2,128)(2,1)}), bf16[2,1024,3,1,128]{4,0,3,2,1:T(2,128)(2,1)}, u32[]{:S(2)}, u32[]{:S(2)}) async-start(bf16[2,1024,3,1,128]{4,0,3,2,1:T(2,128)(2,1)} %copy.228), calls=%async_computation.8 | async-start | bytes 3145728 | tf_op jit(solution)/shard_map/all_to_all | solution.py:290
  365.5 329.8 %all-reduce.4.cloned.1.call-start = ((), (), s32[]{:S(2)}) async-start(), calls=%async_computation.10 | async-start | bytes 33554432 | tf_op jit(solution)/shard_map/psum | solution.py:297
  385.3 23.0 %copy-start.49 = (bf16[2,256,512]{2,1,0:T(8,128)(2,1)S(1)}, bf16[2,256,512]{2,1,0:T(8,128)(2,1)}, u32[]{:S(2)}) copy-start(bf16[2,256,512]{2,1,0:T(8,128)(2,1)} %param.26) | copy-start | bytes 1572868
  (76 other events, 216.7 us)
Sparse Core Ops, SparseCore 0:
  411.2 284.0 all-reduce.3
